TPU v7x, 32 devices: a whole 2x2x4 slice. The times are simulated.
32 devices in a mesh: ctx: 8 (over y, x, core), fsdp: 4 (over z).
Axes of the slice: x: 2, y: 2, z: 4, core: 2. Of those that a mesh axis runs over, the one named last changes fastest.
Arguments:
- tokens: bfloat16 [4, 2048, 2048], P('fsdp', 'ctx'), may hold values from -6 to 6
- qkv_weight: bfloat16 [3, 2048, 2048], P(None, None, 'fsdp'), may hold values from -0.125 to 0.125
- log_decay: float32 [4, 16, 2048], P('fsdp', None, 'ctx'), may hold values from -3 to 0
- norm_gain: float32 [2048], replicated, may hold values from 0.25 to 1.75
Outputs:
- normed: bfloat16 [4, 2048, 2048], P('fsdp', 'ctx')
All inputs are finite; a program needn't handle non-finite values.
Results may differ from a plain program's by a relative error of at most 0.009.
Values may be sent and summed in bfloat16 or wider, within the bound.
A program may use at most 192 MiB of HBM per device.

v0:
```python
import jax
import jax.numpy as jnp
from jax import lax
from jax.sharding import PartitionSpec as P


def entering(part, axis, combine, identity):
    place = lax.axis_index(axis)
    gathered = jax.tree.map(lambda a: lax.all_gather(a, axis), part)
    state = jax.tree.map(lambda a, e: jnp.zeros_like(a) + jnp.asarray(e, a.dtype), part, identity)

    def one(turn, state):
        return combine(
            state, jax.tree.map(lambda a: lax.dynamic_index_in_dim(a, turn, 0, False), gathered)
        )

    return lax.fori_loop(0, place, one, state)


def chain_states(decay_total, local):

    def combine(earlier, later):
        return (earlier[0] * later[0], later[0][:, None, None] * earlier[1] + later[1])

    identity_pair = (jnp.ones_like(decay_total), jnp.zeros_like(local))
    return entering((decay_total, local), "ctx", combine, identity_pair)[1]


def segment_memory_matrix(keys, values, cumulative):
    tail = jnp.exp(cumulative[:, -1:] - cumulative)
    weighted_key_vectors = (keys.astype(jnp.float32) * tail.T[:, :, None]).astype(jnp.bfloat16)
    local = jnp.einsum(
        "thd,the->hde", weighted_key_vectors, values, preferred_element_type=jnp.float32
    )
    return (jnp.exp(cumulative[:, -1]), local)


def body(tokens, qkv_weight, log_decay, norm_gain):
    inputs = tokens[0]
    log_rates = log_decay[0]
    head_count = log_rates.shape[0]
    span_len = log_rates.shape[1]
    feat_total = norm_gain.shape[0]
    head_dimension = feat_total // head_count

    def project(piece):
        return jnp.einsum("td,cde->cte", inputs, piece, preferred_element_type=jnp.float32)

    cumulative = jnp.cumsum(log_rates, axis=1)
    paired = project(lax.all_gather(qkv_weight[1:], "fsdp", axis=2, tiled=True))
    keys = jax.nn.silu(paired[0]).astype(jnp.bfloat16).reshape(span_len, head_count, head_dimension)
    values = paired[1].astype(jnp.bfloat16).reshape(span_len, head_count, head_dimension)
    decay_total, local = segment_memory_matrix(keys, values, cumulative)
    carried = chain_states(decay_total, local)
    asked = project(lax.all_gather(qkv_weight[:1], "fsdp", axis=2, tiled=True))
    queries = (
        jax.nn.silu(asked[0]).astype(jnp.bfloat16).reshape(span_len, head_count, head_dimension)
    )
    log_gaps = cumulative[:, :, None] - cumulative[:, None, :]
    causal = jnp.arange(span_len)[:, None] >= jnp.arange(span_len)[None, :]
    factors = jnp.exp(jnp.where(causal[None], log_gaps, -jnp.inf))
    scores = jnp.einsum("thd,shd->hts", queries, keys, preferred_element_type=jnp.float32)
    weights = (scores * factors).astype(jnp.bfloat16)
    inside = jnp.einsum("hts,shd->thd", weights, values, preferred_element_type=jnp.float32)
    reduced_precision_memory = carried.astype(jnp.bfloat16)
    incoming = jnp.einsum(
        "thd,hde->the", queries, reduced_precision_memory, preferred_element_type=jnp.float32
    )
    incoming = incoming * jnp.exp(cumulative).T[:, :, None]
    attention_output = (inside + incoming).reshape(span_len, feat_total)
    mean_sq = jnp.mean(attention_output * attention_output, axis=-1, keepdims=True)
    normed = (attention_output * lax.rsqrt(mean_sq + 1e-05) * norm_gain).astype(jnp.bfloat16)
    return normed[None]


def solution(mesh):
    placed = (P("fsdp", "ctx", None), P(None, None, "fsdp"), P("fsdp", None, "ctx"), P())
    return jax.shard_map(
        body, mesh=mesh, in_specs=placed, out_specs=P("fsdp", "ctx", None), check_vma=False
    )
```

profile of v0, /device:TPU:7, one launch (start us, length us, event | category | flops | bytes accessed | tf_op | source)
XLA Modules:
  0.0 532.9 jit_solution(12002208312160475600)
XLA Ops:
  6.5 4.5 slice.23
  11.0 6.3 %copy.55 = bf16[2,2048,512]{1,2,0:T(8,128)(2,1)} copy(bf16[2,2048,512]{2,1,0:T(8,128)(2,1)} %slice.23) | data formatting | bytes 8388608
  17.4 3.1 slice.25
  22.3 283.3 %all-gather.6.cloned.1.call-done = bf16[2,2048,2048]{1,2,0:T(8,128)(2,1)} async-done(((bf16[2,2048,512]{1,2,0:T(8,128)(2,1)}), bf16[2,2048,2048]{1,2,0:T(8,128)(2,1)}) %all-gather.6.cloned.1.call-update) | async-done | bytes 16777232 | tf_op jit(solution)/shard_map/all_gather | solution.py:50
  305.7 8.4 %convolution_bitcast_fusion = f32[2,256,2048]{1,2,0:T(8,128)S(1)} fusion(bf16[2,2048,2048]{1,2,0:T(8,128)(2,1)} %all-gather.6.cloned.1.call-done, bf16[1,256,2048]{2,1,0:T(8,128)(2,1)S(1)} %copy-done), kind=kOutput, calls=%fused_computation.5 | convolution fusion | flops 4294967296 | bytes 22020096 | tf_op jit(solution)/shard_map/td,cde->cte/dot_general | solution.py:47
  315.3 1.9 copy.45
  317.2 4.6 fusion.4
  323.4 12.0 %all-reduce = f32[128]{0:T(128)S(1)} all-reduce(f32[128]{0:T(128)S(1)} %dynamic-update-slice), channel_id=2, replica_groups=mesh['ctx'=8,'fsdp'=4] {'ctx'}, use_global_device_ids=true, to_apply=%add | all-reduce | flops 128 | bytes 1024
  335.5 119.6 %all-gather.8.cloned.1.call-done = bf16[1,2048,2048]{2,1,0:T(8,128)(2,1)} async-done(((bf16[1,2048,512]{2,1,0:T(8,128)(2,1)}), bf16[1,2048,2048]{2,1,0:T(8,128)(2,1)}) %all-gather.8.cloned.1.call-update) | async-done | bytes 8388624 | tf_op jit(solution)/shard_map/all_gather | solution.py:55
  455.1 7.2 %fusion = f32[2048,256]{1,0:T(8,128)} fusion(bf16[1,2048,2048]{2,1,0:T(8,128)(2,1)} %all-gather.8.cloned.1.call-done, bf16[1,256,2048]{2,1,0:T(8,128)(2,1)S(1)} %copy-done), kind=kOutput, calls=%fused_computation.2 | convolution fusion | flops 2147483648 | bytes 11534336 | tf_op jit(solution)/shard_map/td,cde->cte/dot_general | solution.py:47
  462.3 2.3 copy.43
  464.5 5.4 %fusion.3 = f32[16,128,256]{2,1,0:T(8,128)} fusion(bf16[256,16,128]{0,2,1:T(8,128)(2,1)S(1)} %bitcast.57, f32[16,256]{1,0:T(8,128)S(1)} %copy_bitcast_fusion, pred[256,256]{1,0:T(8,128)(4,1)S(1)} %iota_compare_fusion, f32[256,16,128]{2,0,1:T(8,128)S(1)} %copy.43, f32[256,16,128]{2,0,1:T(8,128)} %copy.45), kind=kOutput, calls=%fused_computation.14 | convolution fusion | flops 546308096 | bytes 7421952 | tf_op jit(solution)/shard_map/hts,shd->thd/dot_general | solution.py:64
  469.9 38.9 %all-gather.10.cloned.1.call-done = f32[128,128,128]{2,1,0:T(8,128)} async-done(((f32[16,128,128]{2,1,0:T(8,128)}), f32[128,128,128]{2,1,0:T(8,128)}) %all-gather.10.cloned.1.call-update) | async-done | bytes 8388624 | tf_op jit(solution)/shard_map/all_gather | solution.py:9
  509.0 10.5 %while.12 = (s32[]{:T(128)}, f32[16,128,128]{2,1,0:T(8,128)S(1)}, s32[]{:T(128)}, f32[8,16]{1,0:T(8,128)S(1)}, f32[8,16,128,128]{3,2,1,0:T(8,128)}, /*index=5*/s32[]{:T(128)}, s32[]{:T(128)}, s32[]{:T(128)}) while((s32[]{:T(128)}, f32[16,128,128]{2,1,0:T(8,128)S(1)}, s32[]{:T(128)}, f32[8,16]{1,0:T(8,128)S(1)}, f32[8,16,128,128]{3,2,1,0:T(8,128)}, ...), condition=%wide.region_3.4_spmd, body=%wide.region_2.3_spmd.sunk | while | flops 524293 | bytes 3146047 | solution.py:17
  509.0 1.4 bitcast_add_fusion.2
  510.5 1.4 bitcast_add_fusion.2
  512.0 1.4 bitcast_add_fusion.2
  513.5 1.4 bitcast_add_fusion.2
  515.0 1.4 bitcast_add_fusion.2
  516.5 1.4 bitcast_add_fusion.2
  518.0 1.4 bitcast_add_fusion.2
  519.5 3.7 multiply_reduce_fusion
  523.1 2.0 copy.51
  525.2 1.2 multiply_convert_fusion.1
  (43 shorter events, 4.3 us)
Async XLA Ops:
  6.5 299.1 %copy-start = (bf16[1,256,2048]{2,1,0:T(8,128)(2,1)S(1)}, bf16[1,256,2048]{2,1,0:T(8,128)(2,1)}, u32[]{:S(2)}) copy-start(bf16[1,256,2048]{2,1,0:T(8,128)(2,1)} %param.6) | copy-start | bytes 3145732
  6.5 299.1 %all-gather.6.cloned.1.call-start = ((), (), s32[]{:S(2)}) async-start(), calls=%async_computation | async-start | bytes 20971520 | tf_op jit(solution)/shard_map/all_gather | solution.py:50
  17.3 437.8 %all-gather.8.cloned.1.call-start = ((), (), s32[]{:S(2)}) async-start(), calls=%async_computation.1 | async-start | bytes 10485760 | tf_op jit(solution)/shard_map/all_gather | solution.py:55
  20.4 0.7 copy-start.3
  20.5 488.4 %all-gather.10.cloned.1.call-start = ((), (), s32[]{:S(2)}) async-start(), calls=%async_computation.2 | async-start | bytes 9437184 | tf_op jit(solution)/shard_map/all_gather | solution.py:9
  317.2 4.6 copy-start.5
  462.2 2.3 copy-start.2
  523.1 2.0 copy-start.4
  523.1 3.3 copy-start.1
Sparse Core Ops, SparseCore 0:
  17.4 288.1 all-gather.5
  307.2 147.8 all-gather.7
  457.0 51.8 all-gather.9
where the time goes:
time: 534 us; the launch traced here: 533 us
  waiting for transfers between devices  442 us (83%)
  matrix products  29.2 us (5%)
  local copies, waits for them, and re-layouts  23.4 us (4%)
  between operations  13.9 us (3%)
  other arithmetic  12.2 us (2%)
  blocking collectives  12 us (2%)
    all_gather x1, waiting for transfers between devices, body(): paired = project(lax.all_gather(qkv_weight[1:], 'fsdp', axis=2, tiled=True))  283 us
    all_gather x1, waiting for transfers between devices, body(): asked = project(lax.all_gather(qkv_weight[:1], 'fsdp', axis=2, tiled=True))  120 us
    all_gather x1, waiting for transfers between devices, entering(): gathered = jax.tree.map(lambda a: lax.all_gather(a, axis), part)  38.9 us
    dot_general x2, matrix products, project(): jnp.einsum('td,cde->cte', inputs, piece, preferred_element_type=jnp.float32)  15.6 us
    unnamed x1, blocking collectives  12 us
  transfers between devices with their start and end apart: 3, of which 3 were waited for; matrix products, arithmetic and copies ran while one was open for 7% of the time, Pallas kernels for 0%

commit v1 on v0

--- a/solution.py
+++ b/solution.py
@@ -1,7 +1,373 @@
+import functools
 import jax
 import jax.numpy as jnp
 from jax import lax
+from jax.experimental import pallas as pl
+from jax.experimental.pallas import tpu as pltpu
 from jax.sharding import PartitionSpec as P
+
+MESH = pl.DeviceIdType.MESH
+CUBE = 8
+CHUNKS = 4
+F32 = jnp.float32
+BF16 = jnp.bfloat16
+
+
+def flip(c, r):
+    out = c
+    bit = 1
+    while bit < CUBE:
+        if r & bit:
+            out = out + bit - 2 * bit * ((c // bit) % 2)
+        bit *= 2
+    return out
+
+
+def head_kernel(
+    dims,
+    tok_in,
+    w_in,
+    cum_in,
+    gain_ref,
+    out_ref,
+    tok,
+    w,
+    cums,
+    stage,
+    gat,
+    state,
+    local_sem,
+    tok_send,
+    tok_recv,
+    w_up,
+    w_down,
+    w_recv,
+    cum_send,
+    cum_recv,
+    out_send,
+    out_recv,
+):
+    n_fsdp, shard_heads, per_dev, hd, feats = dims
+    groups = n_fsdp // per_dev
+    c = lax.axis_index("ctx")
+    f = lax.axis_index("fsdp")
+    j, a = c // groups, c % groups
+    rows = tok.shape[1]
+    half = rows // 2
+    depth = w.shape[1]
+    step = depth // CHUNKS
+
+    first = jnp.where(f > a * per_dev, 1, 0)
+
+    own_tok = pltpu.make_async_copy(tok_in, tok.at[c], local_sem.at[0])
+    own_tok.start()
+    own_cum = pltpu.make_async_copy(cum_in, cums.at[c], local_sem.at[1])
+    own_cum.start()
+    owner = f // per_dev == a
+    own_i = f % per_dev
+
+    def own_weight(p):
+        return pltpu.make_async_copy(
+            w_in.at[p, :, pl.ds(pl.multiple_of(j * hd, hd), hd)],
+            w.at[own_i, :, pl.ds(p * hd, hd)],
+            local_sem.at[2 + p],
+        )
+
+    @pl.when(owner)
+    def _():
+        for p in range(3):
+            own_weight(p).start()
+
+    barrier = pltpu.get_barrier_semaphore()
+    for r in range(1, CUBE):
+        pl.semaphore_signal(barrier, inc=1, device_id={"ctx": flip(c, r)}, device_id_type=MESH)
+
+    @pl.when(f > 0)
+    def _():
+        pl.semaphore_signal(barrier, inc=1, device_id={"fsdp": f - 1}, device_id_type=MESH)
+
+    @pl.when(f < n_fsdp - 1)
+    def _():
+        pl.semaphore_signal(barrier, inc=1, device_id={"fsdp": f + 1}, device_id_type=MESH)
+
+    ends = jnp.where(f > 0, 1, 0) + jnp.where(f < n_fsdp - 1, 1, 0)
+    pl.semaphore_wait(barrier, CUBE - 1 + ends)
+
+    def tok_copy(r, p, d):
+        part = tok.at[flip(c, r), pl.ds(p * half, half), :]
+        return pltpu.make_async_remote_copy(
+            src_ref=part,
+            dst_ref=part,
+            send_sem=tok_send.at[r, p, (1, 2, 4).index(d)],
+            recv_sem=tok_recv.at[r ^ d, p],
+            device_id={"ctx": flip(c, d)},
+            device_id_type=MESH,
+        )
+
+    def tok_wait(r, p):
+        part = tok.at[flip(c, r), pl.ds(p * half, half), :]
+        pltpu.make_async_remote_copy(
+            src_ref=part,
+            dst_ref=part,
+            send_sem=tok_send.at[r, p, 0],
+            recv_sem=tok_recv.at[r, p],
+            device_id={"ctx": flip(c, 1)},
+            device_id_type=MESH,
+        ).wait_recv()
+
+    sent = []
+
+    def tok_start(r, p, d):
+        copy = tok_copy(r, p, d)
+        copy.start()
+        sent.append(copy)
+
+    def w_copy(i, k, up):
+        part = w.at[i, pl.ds(pl.multiple_of(k * step, step), step), :]
+        return pltpu.make_async_remote_copy(
+            src_ref=part,
+            dst_ref=part,
+            send_sem=(w_up if up else w_down).at[i, k],
+            recv_sem=w_recv.at[i, k],
+            device_id={"fsdp": f + 1 if up else f - 1},
+            device_id_type=MESH,
+        )
+
+    def goes_up(i):
+        return jnp.logical_and(a * per_dev + i <= f, f < n_fsdp - 1)
+
+    def goes_down(i):
+        return jnp.logical_and(a * per_dev + i >= f, f > 0)
+
+    def w_pass(i, k):
+        @pl.when(a * per_dev + i < f)
+        def _():
+            w_copy(i, k, False).wait_recv()
+
+        @pl.when(a * per_dev + i > f)
+        def _():
+            w_copy(i, k, True).wait_recv()
+
+        @pl.when(goes_up(i))
+        def _():
+            w_copy(i, k, True).start()
+
+        @pl.when(goes_down(i))
+        def _():
+            w_copy(i, k, False).start()
+
+    def cum_copy(r):
+        return pltpu.make_async_remote_copy(
+            src_ref=cums.at[c],
+            dst_ref=cums.at[c],
+            send_sem=cum_send.at[r],
+            recv_sem=cum_recv.at[r],
+            device_id={"ctx": flip(c, r)},
+            device_id_type=MESH,
+        )
+
+    @pl.when(owner)
+    def _():
+        for p in range(3):
+            own_weight(p).wait()
+        for k in range(CHUNKS):
+
+            @pl.when(f < n_fsdp - 1)
+            def _():
+                w_copy(own_i, k, True).start()
+
+            @pl.when(f > 0)
+            def _():
+                w_copy(own_i, k, False).start()
+
+    def near_pass(k):
+        @pl.when(a * per_dev + first != f)
+        def _():
+            w_pass(first, k)
+
+    own_cum.wait()
+    own_tok.wait()
+    for p, d in ((0, 2), (1, 4), (1, 2), (0, 4), (0, 1), (1, 1)):
+        tok_start(0, p, d)
+    for r in range(1, CUBE):
+        cum_copy(r).start()
+
+    tok_wait(2, 0)
+    tok_start(2, 0, 4)
+    tok_start(2, 0, 1)
+    tok_wait(4, 1)
+    tok_start(4, 1, 2)
+    tok_start(4, 1, 1)
+    near_pass(0)
+    near_pass(1)
+    tok_wait(2, 1)
+    tok_start(2, 1, 1)
+    tok_wait(4, 0)
+    tok_start(4, 0, 1)
+    near_pass(2)
+    near_pass(3)
+    tok_wait(6, 0)
+    tok_start(6, 0, 1)
+    tok_wait(6, 1)
+    tok_start(6, 1, 1)
+    for r in (1, 3, 5, 7):
+        for p in (0, 1):
+            tok_wait(r, p)
+    for r in range(1, CUBE):
+        pltpu.make_async_remote_copy(
+            src_ref=cums.at[c],
+            dst_ref=cums.at[flip(c, r)],
+            send_sem=cum_send.at[r],
+            recv_sem=cum_recv.at[r],
+            device_id={"ctx": flip(c, r)},
+            device_id_type=MESH,
+        ).wait_recv()
+
+    def head_of(cc, i):
+        return (cc % groups * per_dev + i) * shard_heads + cc // groups
+
+    def columns(cc, i):
+        return pl.ds(pl.multiple_of(head_of(cc, i) * hd, hd), hd)
+
+    def out_copy(i, b):
+        return pltpu.make_async_remote_copy(
+            src_ref=stage.at[i, b],
+            dst_ref=gat.at[:, columns(c, i)],
+            send_sem=out_send.at[i, b],
+            recv_sem=out_recv.at[i, c],
+            device_id={"ctx": b},
+            device_id_type=MESH,
+        )
+
+    t_pos = lax.broadcasted_iota(jnp.int32, (rows, rows), 0)
+    u_pos = lax.broadcasted_iota(jnp.int32, (rows, rows), 1)
+
+    def one(t, _):
+        b = t % CUBE
+        turn = t // CUBE
+        i = first + (1 - 2 * first) * turn
+        far = 1 - first
+
+        @pl.when(t < CHUNKS)
+        def _():
+            w_pass(far, t)
+
+        @pl.when(b == 0)
+        def _():
+            state[...] = jnp.zeros_like(state)
+
+        proj = jnp.dot(tok[b], w[i], preferred_element_type=F32)
+        q = jax.nn.silu(proj[:, :hd]).astype(BF16)
+        k = jax.nn.silu(proj[:, hd : 2 * hd]).astype(BF16)
+        v = proj[:, 2 * hd :].astype(BF16)
+        row = cums[b, pl.ds(head_of(c, i), 1), :]
+        col = jnp.sum(jnp.where(t_pos == u_pos, row, 0.0), axis=1, keepdims=True)
+        total = row[:, rows - 1 :]
+        factors = jnp.exp(jnp.where(t_pos >= u_pos, col - row, -jnp.inf))
+        scores = lax.dot_general(q, k, (((1,), (1,)), ((), ())), preferred_element_type=F32)
+        weights = (scores * factors).astype(BF16)
+        inside = jnp.dot(weights, v, preferred_element_type=F32)
+        held = state[...]
+        incoming = jnp.dot(q, held.astype(BF16), preferred_element_type=F32) * jnp.exp(col)
+        scaled = (k.astype(F32) * jnp.exp(total - col)).astype(BF16)
+        local = lax.dot_general(scaled, v, (((0,), (0,)), ((), ())), preferred_element_type=F32)
+        state[...] = jnp.exp(total) * held + local
+        attended = (inside + incoming).astype(BF16)
+        stage[i, b] = attended
+
+        @pl.when(b == c)
+        def _():
+            gat[:, columns(c, i)] = attended
+
+        @pl.when(b != c)
+        def _():
+            out_copy(i, b).start()
+
+        return 0
+
+    lax.fori_loop(0, per_dev * CUBE, one, 0)
+
+    for copy in sent:
+        copy.wait_send()
+    for r in range(1, CUBE):
+        cum_copy(r).wait_send()
+    for i in range(per_dev):
+        for k in range(CHUNKS):
+
+            @pl.when(goes_up(i))
+            def _():
+                w_copy(i, k, True).wait_send()
+
+            @pl.when(goes_down(i))
+            def _():
+                w_copy(i, k, False).wait_send()
+
+    for i in range(per_dev):
+        for r in range(1, CUBE):
+            peer = flip(c, r)
+            pltpu.make_async_remote_copy(
+                src_ref=stage.at[i, peer],
+                dst_ref=gat.at[:, columns(peer, i)],
+                send_sem=out_send.at[i, peer],
+                recv_sem=out_recv.at[i, peer],
+                device_id={"ctx": peer},
+                device_id_type=MESH,
+            ).wait()
+
+    band = 32
+
+    def norm(n, _):
+        at = pl.ds(pl.multiple_of(n * band, band), band)
+        x = gat[at, :].astype(F32)
+        mean_sq = jnp.sum(x * x, axis=1, keepdims=True) / feats
+        out_ref[at, :] = (x * lax.rsqrt(mean_sq + 1e-05) * gain_ref[...]).astype(BF16)
+        return 0
+
+    lax.fori_loop(0, rows // band, norm, 0)
+
+
+def head_body(n_ctx, n_fsdp, tokens, qkv_weight, log_decay, norm_gain):
+    rows, depth = tokens.shape[1:]
+    heads = log_decay.shape[1]
+    feats = norm_gain.shape[0]
+    hd = feats // heads
+    per_dev = heads // n_ctx
+    cumulative = jnp.cumsum(log_decay[0], axis=1)
+    dims = (n_fsdp, heads // n_fsdp, per_dev, hd, feats)
+    dma = pltpu.SemaphoreType.DMA
+    vmem = pl.BlockSpec(memory_space=pltpu.VMEM)
+    hbm = pl.BlockSpec(memory_space=pl.ANY)
+    normed = pl.pallas_call(
+        functools.partial(head_kernel, dims),
+        out_shape=jax.ShapeDtypeStruct((rows, feats), BF16),
+        in_specs=[hbm, hbm, vmem, vmem],
+        out_specs=vmem,
+        scratch_shapes=[
+            pltpu.VMEM((n_ctx, rows, depth), BF16),
+            pltpu.VMEM((per_dev, depth, 3 * hd), BF16),
+            pltpu.VMEM((n_ctx, heads, rows), F32),
+            pltpu.VMEM((per_dev, n_ctx, rows, hd), BF16),
+            pltpu.VMEM((rows, feats), BF16),
+            pltpu.VMEM((hd, hd), F32),
+            dma((5,)),
+            dma((CUBE, 2, 3)),
+            dma((CUBE, 2)),
+            dma((per_dev, CHUNKS)),
+            dma((per_dev, CHUNKS)),
+            dma((per_dev, CHUNKS)),
+            dma((CUBE,)),
+            dma((CUBE,)),
+            dma((per_dev, n_ctx)),
+            dma((per_dev, n_ctx)),
+        ],
+        compiler_params=pltpu.CompilerParams(
+            collective_id=0, has_side_effects=True, vmem_limit_bytes=56 * 1024 * 1024
+        ),
+        cost_estimate=pl.CostEstimate(
+            flops=6 * rows * depth * feats, bytes_accessed=16 * rows * feats, transcendentals=0
+        ),
+    )(tokens[0], qkv_weight, cumulative, norm_gain[None])
+    return normed[None]
 
 
 def entering(part, axis, combine, identity):
@@ -75,6 +441,14 @@
 
 def solution(mesh):
     placed = (P("fsdp", "ctx", None), P(None, None, "fsdp"), P("fsdp", None, "ctx"), P())
+    n_ctx, n_fsdp = mesh.shape["ctx"], mesh.shape["fsdp"]
+
+    def run(tokens, qkv_weight, log_decay, norm_gain):
+        heads = log_decay.shape[1]
+        by_head = n_ctx == CUBE and heads == 2 * n_ctx and n_fsdp % 2 == 0 and heads % n_fsdp == 0
+        chosen = functools.partial(head_body, n_ctx, n_fsdp) if by_head else body
+        return chosen(tokens, qkv_weight, log_decay, norm_gain)
+
     return jax.shard_map(
-        body, mesh=mesh, in_specs=placed, out_specs=P("fsdp", "ctx", None), check_vma=False
+        run, mesh=mesh, in_specs=placed, out_specs=P("fsdp", "ctx", None), check_vma=False
     )

time: 534 us -> 93.3 us (0.17)
  waiting for transfers between devices: 442 us -> 0 us
  Pallas kernels: 0 us -> 88.4 us
  matrix products: 29.2 us -> 0 us
  local copies, waits for them, and re-layouts: 23.4 us -> 3.2 us
  between operations: 13.9 us -> 0.02 us
  blocking collectives: 12 us -> 0 us
  other arithmetic: 12.2 us -> 1.31 us
    all_gather x3 -> x0, waiting for transfers between devices: 442 us -> none  [the longest x1 283 us: body(): paired = project(lax.all_gather(qkv_weight[1:], 'fsdp', axis=2, tiled=True))]
    pallas_call x0 -> x1, Pallas kernels: none -> 88.4 us  [head_body(): pl.pallas_call(functools.partial(head_kernel, dims), out_shape=jax.ShapeD...]
    dot_general x5 -> x0, matrix products: 29.2 us -> none  [the longest x2 15.6 us: project(): jnp.einsum('td,cde->cte', inputs, piece, preferred_element_type=jnp.float32)]
    unnamed x1 -> x0, blocking collectives: 12 us -> none
    add x7 -> x0, other arithmetic: 10.1 us -> none  [combine(): later[0][:, None, None] * earlier[1] + later[1]]
    slice x6 -> x1, local copies, waits for them, and re-layouts: 9.12 us -> 0.16 us  [the longest x1 4.47 us: body(): paired = project(lax.all_gather(qkv_weight[1:], 'fsdp', axis=2, tiled=True))]
    unnamed x16 -> x1, local copies, waits for them, and re-layouts: 7.83 us -> 2.3 us
  transfers between devices with their start and end apart: 3 -> 0, of which waited for: 3 -> 0; matrix products, arithmetic and copies ran while one was open for 7% -> 0% of each run, Pallas kernels for 0% -> 0%
where the time goes in v1:
time: 93.3 us; the launch traced here: 93 us
  Pallas kernels  88.4 us (95%)
  local copies, waits for them, and re-layouts  3.2 us (3%)
  other arithmetic  1.31 us (1%)
    pallas_call x1, Pallas kernels, head_body(): pl.pallas_call(functools.partial(head_kernel, dims), out_shape=jax.ShapeD...  88.4 us
    unnamed x1, local copies, waits for them, and re-layouts  2.3 us

profile of v1, /device:TPU:7, one launch (start us, length us, event | category | flops | bytes accessed | tf_op | source)
XLA Modules:
  0.0 93.0 jit_solution(1611284721720879549)
XLA Ops:
  0.0 0.7 reshape.11
  0.7 0.6 reduce-window.6
  1.3 0.2 slice_reduce_fusion
  1.5 0.7 copy_bitcast_fusion.cum_in
  2.2 88.4 %shard_map.46 = bf16[256,2048]{1,0:T(8,128)(2,1)} custom-call(bf16[256,2048]{1,0:T(8,128)(2,1)} %bitcast.9, bf16[3,2048,512]{2,1,0:T(8,128)(2,1)} %w_in.1, f32[16,256]{1,0:T(8,128)} %copy_bitcast_fusion.cum_in, f32[1,2048]{1,0:T(1,128)} %bitcast.10), custom_call_target="tpu_custom_call" | custom-call | flops 6442450944 | bytes 8388608 | tf_op jit(solution)/shard_map/pallas_call | solution.py:340
  90.7 2.3 %copy.12 = bf16[1,256,2048]{2,1,0:T(8,128)(2,1)} copy(bf16[1,256,2048]{2,1,0:T(8,128)(2,1)} %bitcast.8) | data formatting | bytes 2097152
  (3 shorter events, 0.0 us)

commit v2 on v1

--- a/solution.py
+++ b/solution.py
@@ -8,7 +8,7 @@
 
 MESH = pl.DeviceIdType.MESH
 CUBE = 8
-CHUNKS = 4
+CHUNKS = 8
 F32 = jnp.float32
 BF16 = jnp.bfloat16
 
@@ -36,6 +36,7 @@
     stage,
     gat,
     state,
+    qkv,
     local_sem,
     tok_send,
     tok_recv,
@@ -180,11 +181,27 @@
             def _():
                 w_copy(own_i, k, False).start()
 
-    def near_pass(k):
-        @pl.when(a * per_dev + first != f)
-        def _():
-            w_pass(first, k)
-
+    inner = jnp.logical_and(f > 0, f < n_fsdp - 1)
+
+    def inner_pass(i, ks):
+        @pl.when(jnp.logical_and(inner, a * per_dev + i != f))
+        def _():
+            for k in ks:
+                w_pass(i, k)
+
+    def end_wait(i):
+        @pl.when(jnp.logical_and(f == 0, a * per_dev + i > f))
+        def _():
+            for k in range(CHUNKS):
+                w_copy(i, k, True).wait_recv()
+
+        @pl.when(jnp.logical_and(f == n_fsdp - 1, a * per_dev + i < f))
+        def _():
+            for k in range(CHUNKS):
+                w_copy(i, k, False).wait_recv()
+
+    far = 1 - first
+    early, late = range(CHUNKS // 2), range(CHUNKS // 2, CHUNKS)
     own_cum.wait()
     own_tok.wait()
     for p, d in ((0, 2), (1, 4), (1, 2), (0, 4), (0, 1), (1, 1)):
@@ -192,24 +209,25 @@
     for r in range(1, CUBE):
         cum_copy(r).start()
 
+    inner_pass(first, early)
     tok_wait(2, 0)
     tok_start(2, 0, 4)
     tok_start(2, 0, 1)
     tok_wait(4, 1)
     tok_start(4, 1, 2)
     tok_start(4, 1, 1)
-    near_pass(0)
-    near_pass(1)
+    inner_pass(first, late)
+    inner_pass(far, early)
     tok_wait(2, 1)
     tok_start(2, 1, 1)
     tok_wait(4, 0)
     tok_start(4, 0, 1)
-    near_pass(2)
-    near_pass(3)
+    inner_pass(far, late)
     tok_wait(6, 0)
     tok_start(6, 0, 1)
     tok_wait(6, 1)
     tok_start(6, 1, 1)
+    end_wait(first)
     for r in (1, 3, 5, 7):
         for p in (0, 1):
             tok_wait(r, p)
@@ -242,50 +260,65 @@
     t_pos = lax.broadcasted_iota(jnp.int32, (rows, rows), 0)
     u_pos = lax.broadcasted_iota(jnp.int32, (rows, rows), 1)
 
-    def one(t, _):
-        b = t % CUBE
+    def place(t):
         turn = t // CUBE
-        i = first + (1 - 2 * first) * turn
-        far = 1 - first
-
-        @pl.when(t < CHUNKS)
-        def _():
-            w_pass(far, t)
+        return first + (1 - 2 * first) * turn, t % CUBE
+
+    def project(t):
+        i, b = place(t)
+        return jnp.dot(tok[b], w[i], preferred_element_type=F32)
+
+    def keep(t, proj):
+        qkv[t % 2, :, : 2 * hd] = jax.nn.silu(proj[:, : 2 * hd]).astype(BF16)
+        qkv[t % 2, :, 2 * hd :] = proj[:, 2 * hd :].astype(BF16)
+
+    def attend(t, ahead):
+        i, b = place(t)
 
         @pl.when(b == 0)
         def _():
             state[...] = jnp.zeros_like(state)
 
-        proj = jnp.dot(tok[b], w[i], preferred_element_type=F32)
-        q = jax.nn.silu(proj[:, :hd]).astype(BF16)
-        k = jax.nn.silu(proj[:, hd : 2 * hd]).astype(BF16)
-        v = proj[:, 2 * hd :].astype(BF16)
+        q = qkv[t % 2, :, :hd]
+        k = qkv[t % 2, :, hd : 2 * hd]
+        v = qkv[t % 2, :, 2 * hd :]
         row = cums[b, pl.ds(head_of(c, i), 1), :]
+        held = state[...]
+        proj = project(t + 1) if ahead else None
         col = jnp.sum(jnp.where(t_pos == u_pos, row, 0.0), axis=1, keepdims=True)
         total = row[:, rows - 1 :]
         factors = jnp.exp(jnp.where(t_pos >= u_pos, col - row, -jnp.inf))
         scores = lax.dot_general(q, k, (((1,), (1,)), ((), ())), preferred_element_type=F32)
         weights = (scores * factors).astype(BF16)
         inside = jnp.dot(weights, v, preferred_element_type=F32)
-        held = state[...]
         incoming = jnp.dot(q, held.astype(BF16), preferred_element_type=F32) * jnp.exp(col)
         scaled = (k.astype(F32) * jnp.exp(total - col)).astype(BF16)
         local = lax.dot_general(scaled, v, (((0,), (0,)), ((), ())), preferred_element_type=F32)
         state[...] = jnp.exp(total) * held + local
         attended = (inside + incoming).astype(BF16)
         stage[i, b] = attended
+        if ahead:
+            keep(t + 1, proj)
 
         @pl.when(b == c)
         def _():
-            gat[:, columns(c, i)] = attended
+            gat[:, columns(c, i)] = stage[i, b]
 
         @pl.when(b != c)
         def _():
             out_copy(i, b).start()
 
+    def one(t, _):
+        @pl.when(t == CUBE - 1)
+        def _():
+            end_wait(far)
+
+        attend(t, True)
         return 0
 
-    lax.fori_loop(0, per_dev * CUBE, one, 0)
+    keep(0, project(0))
+    lax.fori_loop(0, per_dev * CUBE - 1, one, 0)
+    attend(per_dev * CUBE - 1, False)
 
     for copy in sent:
         copy.wait_send()
@@ -349,6 +382,7 @@
             pltpu.VMEM((per_dev, n_ctx, rows, hd), BF16),
             pltpu.VMEM((rows, feats), BF16),
             pltpu.VMEM((hd, hd), F32),
+            pltpu.VMEM((2, rows, 3 * hd), BF16),
             dma((5,)),
             dma((CUBE, 2, 3)),
             dma((CUBE, 2)),

time: 93.3 us -> 76.1 us (0.82)
  Pallas kernels: 88.4 us -> 71.2 us
    pallas_call x1, Pallas kernels: 88.4 us -> 71.2 us  [head_body(): pl.pallas_call(functools.partial(head_kernel, dims), out_shape=jax.ShapeD...]
where the time goes in v2:
time: 76.1 us; the launch traced here: 75.7 us
  Pallas kernels  71.2 us (94%)
  local copies, waits for them, and re-layouts  3.2 us (4%)
  other arithmetic  1.31 us (2%)
    pallas_call x1, Pallas kernels, head_body(): pl.pallas_call(functools.partial(head_kernel, dims), out_shape=jax.ShapeD...  71.2 us
    unnamed x1, local copies, waits for them, and re-layouts  2.3 us

profile of v2, /device:TPU:7, one launch (start us, length us, event | category | flops | bytes accessed | tf_op | source)
XLA Modules:
  0.0 75.7 jit_solution(7107598458402249650)
XLA Ops:
  0.0 0.7 reshape.11
  0.7 0.6 reduce-window.6
  1.3 0.2 slice_reduce_fusion
  1.5 0.7 copy_bitcast_fusion.cum_in
  2.2 71.2 %shard_map.46 = bf16[256,2048]{1,0:T(8,128)(2,1)} custom-call(bf16[256,2048]{1,0:T(8,128)(2,1)} %bitcast.9, bf16[3,2048,512]{2,1,0:T(8,128)(2,1)} %w_in.1, f32[16,256]{1,0:T(8,128)} %copy_bitcast_fusion.cum_in, f32[1,2048]{1,0:T(1,128)} %bitcast.10), custom_call_target="tpu_custom_call" | custom-call | flops 6442450944 | bytes 8388608 | tf_op jit(solution)/shard_map/pallas_call | solution.py:373
  73.4 2.3 %copy.12 = bf16[1,256,2048]{2,1,0:T(8,128)(2,1)} copy(bf16[1,256,2048]{2,1,0:T(8,128)(2,1)} %bitcast.8) | data formatting | bytes 2097152
  (3 shorter events, 0.0 us)

commit v3 on v2

--- a/solution.py
+++ b/solution.py
@@ -27,7 +27,7 @@
     dims,
     tok_in,
     w_in,
-    cum_in,
+    decay_in,
     gain_ref,
     out_ref,
     tok,
@@ -36,7 +36,13 @@
     stage,
     gat,
     state,
-    qkv,
+    sums,
+    factors,
+    opening,
+    closing,
+    near_qkv,
+    far_qkv,
+    partial,
     local_sem,
     tok_send,
     tok_recv,
@@ -60,10 +66,9 @@
 
     first = jnp.where(f > a * per_dev, 1, 0)
 
-    own_tok = pltpu.make_async_copy(tok_in, tok.at[c], local_sem.at[0])
+    own_tok = pltpu.make_async_copy(tok_in.at[0], tok.at[c], local_sem.at[0])
     own_tok.start()
-    own_cum = pltpu.make_async_copy(cum_in, cums.at[c], local_sem.at[1])
-    own_cum.start()
+    cums[c] = decay_in[0]
     owner = f // per_dev == a
     own_i = f % per_dev
 
@@ -71,7 +76,7 @@
         return pltpu.make_async_copy(
             w_in.at[p, :, pl.ds(pl.multiple_of(j * hd, hd), hd)],
             w.at[own_i, :, pl.ds(p * hd, hd)],
-            local_sem.at[2 + p],
+            local_sem.at[1 + p],
         )
 
     @pl.when(owner)
@@ -159,7 +164,7 @@
 
     def cum_copy(r):
         return pltpu.make_async_remote_copy(
-            src_ref=cums.at[c],
+            src_ref=decay_in.at[0],
             dst_ref=cums.at[c],
             send_sem=cum_send.at[r],
             recv_sem=cum_recv.at[r],
@@ -167,6 +172,13 @@
             device_id_type=MESH,
         )
 
+    for r in range(1, CUBE):
+        cum_copy(r).start()
+
+    own_tok.wait()
+    for p, d in ((0, 2), (1, 4), (1, 2), (0, 4), (0, 1), (1, 1)):
+        tok_start(0, p, d)
+
     @pl.when(owner)
     def _():
         for p in range(3):
@@ -189,25 +201,79 @@
             for k in ks:
                 w_pass(i, k)
 
-    def end_wait(i):
+    def end_wait(i, ks):
         @pl.when(jnp.logical_and(f == 0, a * per_dev + i > f))
         def _():
-            for k in range(CHUNKS):
+            for k in ks:
                 w_copy(i, k, True).wait_recv()
 
         @pl.when(jnp.logical_and(f == n_fsdp - 1, a * per_dev + i < f))
         def _():
-            for k in range(CHUNKS):
+            for k in ks:
                 w_copy(i, k, False).wait_recv()
 
     far = 1 - first
     early, late = range(CHUNKS // 2), range(CHUNKS // 2, CHUNKS)
-    own_cum.wait()
-    own_tok.wait()
-    for p, d in ((0, 2), (1, 4), (1, 2), (0, 4), (0, 1), (1, 1)):
-        tok_start(0, p, d)
+    def head_of(cc, i):
+        return (cc % groups * per_dev + i) * shard_heads + cc // groups
+
+    def columns(cc, i):
+        return pl.ds(pl.multiple_of(head_of(cc, i) * hd, hd), hd)
+
+    def out_copy(i, b):
+        return pltpu.make_async_remote_copy(
+            src_ref=stage.at[i, b],
+            dst_ref=gat.at[:, columns(c, i)],
+            send_sem=out_send.at[i, b],
+            recv_sem=out_recv.at[i, c],
+            device_id={"ctx": b},
+            device_id_type=MESH,
+        )
+
     for r in range(1, CUBE):
-        cum_copy(r).start()
+        pltpu.make_async_remote_copy(
+            src_ref=decay_in.at[0],
+            dst_ref=cums.at[flip(c, r)],
+            send_sem=cum_send.at[r],
+            recv_sem=cum_recv.at[r],
+            device_id={"ctx": flip(c, r)},
+            device_id_type=MESH,
+        ).wait_recv()
+
+    t_pos = lax.broadcasted_iota(jnp.int32, (rows, rows), 0)
+    u_pos = lax.broadcasted_iota(jnp.int32, (rows, rows), 1)
+    upto = jnp.where(t_pos <= u_pos, 1.0, 0.0).astype(F32)
+    for i in range(per_dev):
+        rates = jnp.concatenate(
+            [cums[b, pl.ds(head_of(c, i), 1), :] for b in range(CUBE)], axis=0
+        )
+        sums[i] = jnp.dot(
+            rates, upto, preferred_element_type=F32, precision=lax.Precision.HIGHEST
+        )
+
+    def decays(n, _):
+        i, b = n // CUBE, n % CUBE
+        row = sums[i, pl.ds(b, 1), :]
+        col = jnp.sum(jnp.where(t_pos == u_pos, row, 0.0), axis=1, keepdims=True)
+        factors[i, b] = jnp.exp(jnp.where(t_pos >= u_pos, col - row, -jnp.inf))
+        opening[i, b] = jnp.broadcast_to(jnp.exp(col), (rows, hd))
+        closing[i, b] = jnp.broadcast_to(jnp.exp(row[:, rows - 1 :] - col), (rows, hd))
+        return 0
+
+    lax.fori_loop(0, per_dev * CUBE, decays, 0)
+
+    def activate(proj):
+        qk = jax.nn.silu(proj[:, : 2 * hd]).astype(BF16)
+        return jnp.concatenate([qk, proj[:, 2 * hd :].astype(BF16)], axis=1)
+
+    def near_project(r, _):
+        b = c
+        bit = 1
+        while bit < CUBE:
+            b = b + ((r // bit) % 2) * (bit - 2 * bit * ((c // bit) % 2))
+            bit *= 2
+        near_qkv[b] = activate(jnp.dot(tok[b], w[first], preferred_element_type=F32))
+        return 0
 
     inner_pass(first, early)
     tok_wait(2, 0)
@@ -223,82 +289,38 @@
     tok_wait(4, 0)
     tok_start(4, 0, 1)
     inner_pass(far, late)
+    end_wait(first, range(CHUNKS))
+    for r in (1, 3, 5):
+        for p in (0, 1):
+            tok_wait(r, p)
+    lax.fori_loop(0, 6, near_project, 0)
     tok_wait(6, 0)
     tok_start(6, 0, 1)
     tok_wait(6, 1)
     tok_start(6, 1, 1)
-    end_wait(first)
-    for r in (1, 3, 5, 7):
-        for p in (0, 1):
-            tok_wait(r, p)
-    for r in range(1, CUBE):
-        pltpu.make_async_remote_copy(
-            src_ref=cums.at[c],
-            dst_ref=cums.at[flip(c, r)],
-            send_sem=cum_send.at[r],
-            recv_sem=cum_recv.at[r],
-            device_id={"ctx": flip(c, r)},
-            device_id_type=MESH,
-        ).wait_recv()
-
-    def head_of(cc, i):
-        return (cc % groups * per_dev + i) * shard_heads + cc // groups
-
-    def columns(cc, i):
-        return pl.ds(pl.multiple_of(head_of(cc, i) * hd, hd), hd)
-
-    def out_copy(i, b):
-        return pltpu.make_async_remote_copy(
-            src_ref=stage.at[i, b],
-            dst_ref=gat.at[:, columns(c, i)],
-            send_sem=out_send.at[i, b],
-            recv_sem=out_recv.at[i, c],
-            device_id={"ctx": b},
-            device_id_type=MESH,
-        )
-
-    t_pos = lax.broadcasted_iota(jnp.int32, (rows, rows), 0)
-    u_pos = lax.broadcasted_iota(jnp.int32, (rows, rows), 1)
-
-    def place(t):
-        turn = t // CUBE
-        return first + (1 - 2 * first) * turn, t % CUBE
-
-    def project(t):
-        i, b = place(t)
-        return jnp.dot(tok[b], w[i], preferred_element_type=F32)
-
-    def keep(t, proj):
-        qkv[t % 2, :, : 2 * hd] = jax.nn.silu(proj[:, : 2 * hd]).astype(BF16)
-        qkv[t % 2, :, 2 * hd :] = proj[:, 2 * hd :].astype(BF16)
-
-    def attend(t, ahead):
-        i, b = place(t)
+    for p in (0, 1):
+        tok_wait(7, p)
+    lax.fori_loop(6, CUBE, near_project, 0)
+
+    def attend(i, b, qkv, ahead):
+        q, k, v = qkv[:, :hd], qkv[:, hd : 2 * hd], qkv[:, 2 * hd :]
 
         @pl.when(b == 0)
         def _():
             state[...] = jnp.zeros_like(state)
 
-        q = qkv[t % 2, :, :hd]
-        k = qkv[t % 2, :, hd : 2 * hd]
-        v = qkv[t % 2, :, 2 * hd :]
-        row = cums[b, pl.ds(head_of(c, i), 1), :]
         held = state[...]
-        proj = project(t + 1) if ahead else None
-        col = jnp.sum(jnp.where(t_pos == u_pos, row, 0.0), axis=1, keepdims=True)
-        total = row[:, rows - 1 :]
-        factors = jnp.exp(jnp.where(t_pos >= u_pos, col - row, -jnp.inf))
+        if ahead is not None:
+            ahead()
         scores = lax.dot_general(q, k, (((1,), (1,)), ((), ())), preferred_element_type=F32)
-        weights = (scores * factors).astype(BF16)
+        weights = (scores * factors[i, b]).astype(BF16)
         inside = jnp.dot(weights, v, preferred_element_type=F32)
-        incoming = jnp.dot(q, held.astype(BF16), preferred_element_type=F32) * jnp.exp(col)
-        scaled = (k.astype(F32) * jnp.exp(total - col)).astype(BF16)
+        incoming = jnp.dot(q, held.astype(BF16), preferred_element_type=F32) * opening[i, b]
+        scaled = (k.astype(F32) * closing[i, b]).astype(BF16)
         local = lax.dot_general(scaled, v, (((0,), (0,)), ((), ())), preferred_element_type=F32)
-        state[...] = jnp.exp(total) * held + local
-        attended = (inside + incoming).astype(BF16)
-        stage[i, b] = attended
-        if ahead:
-            keep(t + 1, proj)
+        total = jnp.exp(sums[i, pl.ds(b, 1), :][:, rows - 1 :])
+        state[...] = total * held + local
+        stage[i, b] = (inside + incoming).astype(BF16)
 
         @pl.when(b == c)
         def _():
@@ -308,17 +330,42 @@
         def _():
             out_copy(i, b).start()
 
-    def one(t, _):
-        @pl.when(t == CUBE - 1)
-        def _():
-            end_wait(far)
-
-        attend(t, True)
-        return 0
-
-    keep(0, project(0))
-    lax.fori_loop(0, per_dev * CUBE - 1, one, 0)
-    attend(per_dev * CUBE - 1, False)
+    def near_one(b, _):
+        attend(first, b, near_qkv[b], None)
+        return 0
+
+    lax.fori_loop(0, CUBE, near_one, 0)
+
+    def piece(b, lo, hi):
+        at = pl.ds(lo * step, (hi - lo) * step)
+        return jnp.dot(tok[b, :, at], w[far, at, :], preferred_element_type=F32)
+
+    half_way, most = CHUNKS // 2, CHUNKS - CHUNKS // 4
+
+    def grow_first(b, _):
+        partial[b] = piece(b, 0, half_way)
+        return 0
+
+    def grow_next(b, _):
+        partial[b] += piece(b, half_way, most)
+        return 0
+
+    def finish(b):
+        far_qkv[b % 2] = activate(partial[b] + piece(b, most, CHUNKS))
+
+    end_wait(far, range(half_way))
+    lax.fori_loop(0, CUBE, grow_first, 0)
+    end_wait(far, range(half_way, most))
+    lax.fori_loop(0, CUBE, grow_next, 0)
+    end_wait(far, range(most, CHUNKS))
+    finish(0)
+
+    def far_one(b, _):
+        attend(far, b, far_qkv[b % 2], functools.partial(finish, b + 1))
+        return 0
+
+    lax.fori_loop(0, CUBE - 1, far_one, 0)
+    attend(far, CUBE - 1, far_qkv[(CUBE - 1) % 2], None)
 
     for copy in sent:
         copy.wait_send()
@@ -353,7 +400,7 @@
         at = pl.ds(pl.multiple_of(n * band, band), band)
         x = gat[at, :].astype(F32)
         mean_sq = jnp.sum(x * x, axis=1, keepdims=True) / feats
-        out_ref[at, :] = (x * lax.rsqrt(mean_sq + 1e-05) * gain_ref[...]).astype(BF16)
+        out_ref[0, at, :] = (x * lax.rsqrt(mean_sq + 1e-05) * gain_ref[...]).astype(BF16)
         return 0
 
     lax.fori_loop(0, rows // band, norm, 0)
@@ -365,14 +412,13 @@
     feats = norm_gain.shape[0]
     hd = feats // heads
     per_dev = heads // n_ctx
-    cumulative = jnp.cumsum(log_decay[0], axis=1)
     dims = (n_fsdp, heads // n_fsdp, per_dev, hd, feats)
     dma = pltpu.SemaphoreType.DMA
     vmem = pl.BlockSpec(memory_space=pltpu.VMEM)
     hbm = pl.BlockSpec(memory_space=pl.ANY)
     normed = pl.pallas_call(
         functools.partial(head_kernel, dims),
-        out_shape=jax.ShapeDtypeStruct((rows, feats), BF16),
+        out_shape=jax.ShapeDtypeStruct((1, rows, feats), BF16),
         in_specs=[hbm, hbm, vmem, vmem],
         out_specs=vmem,
         scratch_shapes=[
@@ -382,8 +428,14 @@
             pltpu.VMEM((per_dev, n_ctx, rows, hd), BF16),
             pltpu.VMEM((rows, feats), BF16),
             pltpu.VMEM((hd, hd), F32),
+            pltpu.VMEM((per_dev, n_ctx, rows), F32),
+            pltpu.VMEM((per_dev, n_ctx, rows, rows), F32),
+            pltpu.VMEM((per_dev, n_ctx, rows, hd), F32),
+            pltpu.VMEM((per_dev, n_ctx, rows, hd), F32),
+            pltpu.VMEM((n_ctx, rows, 3 * hd), BF16),
             pltpu.VMEM((2, rows, 3 * hd), BF16),
-            dma((5,)),
+            pltpu.VMEM((n_ctx, rows, 3 * hd), F32),
+            dma((4,)),
             dma((CUBE, 2, 3)),
             dma((CUBE, 2)),
             dma((per_dev, CHUNKS)),
@@ -400,8 +452,8 @@
         cost_estimate=pl.CostEstimate(
             flops=6 * rows * depth * feats, bytes_accessed=16 * rows * feats, transcendentals=0
         ),
-    )(tokens[0], qkv_weight, cumulative, norm_gain[None])
-    return normed[None]
+    )(tokens, qkv_weight, log_decay, norm_gain[None])
+    return normed
 
 
 def entering(part, axis, combine, identity):

time: 76.1 us -> 72.9 us (0.958)
  other arithmetic: 1.31 us -> 0 us
  Pallas kernels: 71.2 us -> 70 us
  local copies, waits for them, and re-layouts: 3.2 us -> 2.3 us
    another operation x3 -> x0, other arithmetic: 1.31 us -> none
    pallas_call x1, Pallas kernels: 71.2 us -> 70 us  [head_body(): pl.pallas_call(functools.partial(head_kernel, dims), out_shape=jax.ShapeD...]
where the time goes in v3:
time: 72.9 us; the launch traced here: 72.3 us
  Pallas kernels  70 us (96%)
  local copies, waits for them, and re-layouts  2.3 us (3%)
    pallas_call x1, Pallas kernels, head_body(): pl.pallas_call(functools.partial(head_kernel, dims), out_shape=jax.ShapeD...  70 us
    unnamed x1, local copies, waits for them, and re-layouts  2.3 us

profile of v3, /device:TPU:7, one launch (start us, length us, event | category | flops | bytes accessed | tf_op | source)
XLA Modules:
  0.0 72.3 jit_solution(8240391260084748929)
XLA Ops:
  0.0 70.0 %shard_map.46 = bf16[1,256,2048]{2,1,0:T(8,128)(2,1)} custom-call(bf16[1,256,2048]{2,1,0:T(8,128)(2,1)} %tok_in.1, bf16[3,2048,512]{2,1,0:T(8,128)(2,1)} %w_in.1, f32[1,16,256]{2,1,0:T(8,128)} %decay_in.1, f32[1,2048]{1,0:T(1,128)} %bitcast.1), custom_call_target="tpu_custom_call" | custom-call | flops 6442450944 | bytes 8388608 | tf_op jit(solution)/shard_map/pallas_call | solution.py:419
  70.0 2.3 %copy.6 = bf16[1,256,2048]{2,1,0:T(8,128)(2,1)} copy(bf16[1,256,2048]{2,1,0:T(8,128)(2,1)} %shard_map.46) | data formatting | bytes 2097152

commit v4 on v3

--- a/solution.py
+++ b/solution.py
@@ -40,7 +40,9 @@
     factors,
     opening,
     closing,
-    near_qkv,
+    near_q,
+    near_inside,
+    near_local,
     far_qkv,
     partial,
     local_sem,
@@ -176,14 +178,8 @@
         cum_copy(r).start()
 
     own_tok.wait()
-    for p, d in ((0, 2), (1, 4), (1, 2), (0, 4), (0, 1), (1, 1)):
-        tok_start(0, p, d)
-
-    @pl.when(owner)
-    def _():
-        for p in range(3):
-            own_weight(p).wait()
-        for k in range(CHUNKS):
+    def own_start(ks):
+        for k in ks:
 
             @pl.when(f < n_fsdp - 1)
             def _():
@@ -192,6 +188,25 @@
             @pl.when(f > 0)
             def _():
                 w_copy(own_i, k, False).start()
+
+    tok_start(0, 0, 2)
+    tok_start(0, 1, 4)
+
+    @pl.when(owner)
+    def _():
+        for p in range(3):
+            own_weight(p).wait()
+        own_start(range(CHUNKS // 2))
+
+    tok_start(0, 1, 2)
+    tok_start(0, 0, 4)
+
+    @pl.when(owner)
+    def _():
+        own_start(range(CHUNKS // 2, CHUNKS))
+
+    tok_start(0, 0, 1)
+    tok_start(0, 1, 1)
 
     inner = jnp.logical_and(f > 0, f < n_fsdp - 1)
 
@@ -230,6 +245,89 @@
             device_id_type=MESH,
         )
 
+    t_pos = lax.broadcasted_iota(jnp.int32, (rows, rows), 0)
+    u_pos = lax.broadcasted_iota(jnp.int32, (rows, rows), 1)
+    def decays(n, _):
+        i, b = n // CUBE, n % CUBE
+        row = sums[i, pl.ds(b, 1), :]
+        col = jnp.sum(jnp.where(t_pos == u_pos, row, 0.0), axis=1, keepdims=True)
+        factors[i, b] = jnp.exp(jnp.where(t_pos >= u_pos, col - row, -jnp.inf))
+        opening[i, b] = jnp.broadcast_to(jnp.exp(col), (rows, hd))
+        closing[i, b] = jnp.broadcast_to(jnp.exp(row[:, rows - 1 :] - col), (rows, hd))
+        return 0
+
+    def activate(proj):
+        qk = jax.nn.silu(proj[:, : 2 * hd]).astype(BF16)
+        return jnp.concatenate([qk, proj[:, 2 * hd :].astype(BF16)], axis=1)
+
+    def flipped(r):
+        b = c
+        bit = 1
+        while bit < CUBE:
+            b = b + ((r // bit) % 2) * (bit - 2 * bit * ((c // bit) % 2))
+            bit *= 2
+        return b
+
+    def block_alone(i, b, qkv):
+        q, k, v = qkv[:, :hd], qkv[:, hd : 2 * hd], qkv[:, 2 * hd :]
+        scores = lax.dot_general(q, k, (((1,), (1,)), ((), ())), preferred_element_type=F32)
+        weights = (scores * factors[i, b]).astype(BF16)
+        inside = jnp.dot(weights, v, preferred_element_type=F32)
+        scaled = (k.astype(F32) * closing[i, b]).astype(BF16)
+        local = lax.dot_general(scaled, v, (((0,), (0,)), ((), ())), preferred_element_type=F32)
+        return inside, local
+
+    def chain(i, b, held, q, inside, local):
+        incoming = jnp.dot(q, held.astype(BF16), preferred_element_type=F32) * opening[i, b]
+        total = jnp.exp(sums[i, pl.ds(b, 1), :][:, rows - 1 :])
+        state[...] = total * held + local
+        stage[i, b] = (inside + incoming).astype(BF16)
+
+    def send(i, b):
+        @pl.when(b == c)
+        def _():
+            gat[:, columns(c, i)] = stage[i, b]
+
+        @pl.when(b != c)
+        def _():
+            out_copy(i, b).start()
+
+    def near_block(r, _):
+        b = flipped(r)
+        qkv = activate(jnp.dot(tok[b], w[first], preferred_element_type=F32))
+        near_q[b] = qkv[:, :hd]
+        near_inside[b], near_local[b] = block_alone(first, b, qkv)
+        return 0
+
+    def piece(b, lo, hi):
+        at = pl.ds(lo * step, (hi - lo) * step)
+        return jnp.dot(tok[b, :, at], w[far, at, :], preferred_element_type=F32)
+
+    half_way, most = CHUNKS // 2, CHUNKS - CHUNKS // 4
+
+    def grow(r, _):
+        b = flipped(r)
+        partial[b] = piece(b, 0, most)
+        return 0
+
+    def grow_first(b, _):
+        partial[b] = piece(b, 0, half_way)
+        return 0
+
+    def grow_next(b, _):
+        partial[b] += piece(b, half_way, most)
+        return 0
+
+    def finish(b):
+        far_qkv[b % 2] = activate(partial[b] + piece(b, most, CHUNKS))
+
+    inner_pass(first, early)
+    tok_wait(2, 0)
+    tok_start(2, 0, 4)
+    tok_start(2, 0, 1)
+    tok_wait(4, 1)
+    tok_start(4, 1, 2)
+    tok_start(4, 1, 1)
     for r in range(1, CUBE):
         pltpu.make_async_remote_copy(
             src_ref=decay_in.at[0],
@@ -240,8 +338,6 @@
             device_id_type=MESH,
         ).wait_recv()
 
-    t_pos = lax.broadcasted_iota(jnp.int32, (rows, rows), 0)
-    u_pos = lax.broadcasted_iota(jnp.int32, (rows, rows), 1)
     upto = jnp.where(t_pos <= u_pos, 1.0, 0.0).astype(F32)
     for i in range(per_dev):
         rates = jnp.concatenate(
@@ -251,37 +347,7 @@
             rates, upto, preferred_element_type=F32, precision=lax.Precision.HIGHEST
         )
 
-    def decays(n, _):
-        i, b = n // CUBE, n % CUBE
-        row = sums[i, pl.ds(b, 1), :]
-        col = jnp.sum(jnp.where(t_pos == u_pos, row, 0.0), axis=1, keepdims=True)
-        factors[i, b] = jnp.exp(jnp.where(t_pos >= u_pos, col - row, -jnp.inf))
-        opening[i, b] = jnp.broadcast_to(jnp.exp(col), (rows, hd))
-        closing[i, b] = jnp.broadcast_to(jnp.exp(row[:, rows - 1 :] - col), (rows, hd))
-        return 0
-
     lax.fori_loop(0, per_dev * CUBE, decays, 0)
-
-    def activate(proj):
-        qk = jax.nn.silu(proj[:, : 2 * hd]).astype(BF16)
-        return jnp.concatenate([qk, proj[:, 2 * hd :].astype(BF16)], axis=1)
-
-    def near_project(r, _):
-        b = c
-        bit = 1
-        while bit < CUBE:
-            b = b + ((r // bit) % 2) * (bit - 2 * bit * ((c // bit) % 2))
-            bit *= 2
-        near_qkv[b] = activate(jnp.dot(tok[b], w[first], preferred_element_type=F32))
-        return 0
-
-    inner_pass(first, early)
-    tok_wait(2, 0)
-    tok_start(2, 0, 4)
-    tok_start(2, 0, 1)
-    tok_wait(4, 1)
-    tok_start(4, 1, 2)
-    tok_start(4, 1, 1)
     inner_pass(first, late)
     inner_pass(far, early)
     tok_wait(2, 1)
@@ -293,79 +359,58 @@
     for r in (1, 3, 5):
         for p in (0, 1):
             tok_wait(r, p)
-    lax.fori_loop(0, 6, near_project, 0)
+    lax.fori_loop(0, 6, near_block, 0)
+
+    @pl.when(inner)
+    def _():
+        lax.fori_loop(0, 6, grow, 0)
+
     tok_wait(6, 0)
     tok_start(6, 0, 1)
     tok_wait(6, 1)
     tok_start(6, 1, 1)
     for p in (0, 1):
         tok_wait(7, p)
-    lax.fori_loop(6, CUBE, near_project, 0)
-
-    def attend(i, b, qkv, ahead):
-        q, k, v = qkv[:, :hd], qkv[:, hd : 2 * hd], qkv[:, 2 * hd :]
-
-        @pl.when(b == 0)
-        def _():
-            state[...] = jnp.zeros_like(state)
-
-        held = state[...]
-        if ahead is not None:
-            ahead()
-        scores = lax.dot_general(q, k, (((1,), (1,)), ((), ())), preferred_element_type=F32)
-        weights = (scores * factors[i, b]).astype(BF16)
-        inside = jnp.dot(weights, v, preferred_element_type=F32)
-        incoming = jnp.dot(q, held.astype(BF16), preferred_element_type=F32) * opening[i, b]
-        scaled = (k.astype(F32) * closing[i, b]).astype(BF16)
-        local = lax.dot_general(scaled, v, (((0,), (0,)), ((), ())), preferred_element_type=F32)
-        total = jnp.exp(sums[i, pl.ds(b, 1), :][:, rows - 1 :])
-        state[...] = total * held + local
-        stage[i, b] = (inside + incoming).astype(BF16)
-
-        @pl.when(b == c)
-        def _():
-            gat[:, columns(c, i)] = stage[i, b]
-
-        @pl.when(b != c)
-        def _():
-            out_copy(i, b).start()
+    lax.fori_loop(6, CUBE, near_block, 0)
+
+    state[...] = jnp.zeros_like(state)
 
     def near_one(b, _):
-        attend(first, b, near_qkv[b], None)
+        chain(first, b, state[...], near_q[b], near_inside[b], near_local[b])
+        send(first, b)
         return 0
 
     lax.fori_loop(0, CUBE, near_one, 0)
 
-    def piece(b, lo, hi):
-        at = pl.ds(lo * step, (hi - lo) * step)
-        return jnp.dot(tok[b, :, at], w[far, at, :], preferred_element_type=F32)
-
-    half_way, most = CHUNKS // 2, CHUNKS - CHUNKS // 4
-
-    def grow_first(b, _):
-        partial[b] = piece(b, 0, half_way)
-        return 0
-
-    def grow_next(b, _):
-        partial[b] += piece(b, half_way, most)
-        return 0
-
-    def finish(b):
-        far_qkv[b % 2] = activate(partial[b] + piece(b, most, CHUNKS))
-
-    end_wait(far, range(half_way))
-    lax.fori_loop(0, CUBE, grow_first, 0)
-    end_wait(far, range(half_way, most))
-    lax.fori_loop(0, CUBE, grow_next, 0)
-    end_wait(far, range(most, CHUNKS))
+    @pl.when(inner)
+    def _():
+        lax.fori_loop(6, CUBE, grow, 0)
+
+    @pl.when(jnp.logical_not(inner))
+    def _():
+        end_wait(far, range(half_way))
+        lax.fori_loop(0, CUBE, grow_first, 0)
+        end_wait(far, range(half_way, most))
+        lax.fori_loop(0, CUBE, grow_next, 0)
+        end_wait(far, range(most, CHUNKS))
+
     finish(0)
+    state[...] = jnp.zeros_like(state)
+
+    def far_block(b, ahead):
+        qkv, held = far_qkv[b % 2], state[...]
+        if ahead:
+            finish(b + 1)
+        inside, local = block_alone(far, b, qkv)
+        chain(far, b, held, qkv[:, :hd], inside, local)
+        send(far, b)
 
     def far_one(b, _):
-        attend(far, b, far_qkv[b % 2], functools.partial(finish, b + 1))
+        far_block(b, True)
         return 0
 
     lax.fori_loop(0, CUBE - 1, far_one, 0)
-    attend(far, CUBE - 1, far_qkv[(CUBE - 1) % 2], None)
+    far_block(CUBE - 1, False)
 
     for copy in sent:
         copy.wait_send()
@@ -432,7 +477,9 @@
             pltpu.VMEM((per_dev, n_ctx, rows, rows), F32),
             pltpu.VMEM((per_dev, n_ctx, rows, hd), F32),
             pltpu.VMEM((per_dev, n_ctx, rows, hd), F32),
-            pltpu.VMEM((n_ctx, rows, 3 * hd), BF16),
+            pltpu.VMEM((n_ctx, rows, hd), BF16),
+            pltpu.VMEM((n_ctx, rows, hd), F32),
+            pltpu.VMEM((n_ctx, hd, hd), F32),
             pltpu.VMEM((2, rows, 3 * hd), BF16),
             pltpu.VMEM((n_ctx, rows, 3 * hd), F32),
             dma((4,)),

time: 72.9 us -> 73.2 us (level)
  no operation moved by 1% of the time
where the time goes in v4:
time: 73.2 us; the launch traced here: 72.2 us
  Pallas kernels  69.9 us (95%)
  local copies, waits for them, and re-layouts  2.3 us (3%)
    pallas_call x1, Pallas kernels, head_body(): pl.pallas_call(functools.partial(head_kernel, dims), out_shape=jax.ShapeD...  69.9 us
    unnamed x1, local copies, waits for them, and re-layouts  2.3 us

profile of v4, /device:TPU:7, one launch (start us, length us, event | category | flops | bytes accessed | tf_op | source)
XLA Modules:
  0.0 72.2 jit_solution(10751022270179556786)
XLA Ops:
  0.0 69.9 %shard_map.46 = bf16[1,256,2048]{2,1,0:T(8,128)(2,1)} custom-call(bf16[1,256,2048]{2,1,0:T(8,128)(2,1)} %tok_in.1, bf16[3,2048,512]{2,1,0:T(8,128)(2,1)} %w_in.1, f32[1,16,256]{2,1,0:T(8,128)} %decay_in.1, f32[1,2048]{1,0:T(1,128)} %bitcast.1), custom_call_target="tpu_custom_call" | custom-call | flops 6442450944 | bytes 8388608 | tf_op jit(solution)/shard_map/pallas_call | solution.py:464
  69.9 2.3 %copy.6 = bf16[1,256,2048]{2,1,0:T(8,128)(2,1)} copy(bf16[1,256,2048]{2,1,0:T(8,128)(2,1)} %shard_map.46) | data formatting | bytes 2097152

commit v5 on v4

--- a/solution.py
+++ b/solution.py
@@ -189,24 +189,14 @@
             def _():
                 w_copy(own_i, k, False).start()
 
-    tok_start(0, 0, 2)
-    tok_start(0, 1, 4)
-
     @pl.when(owner)
     def _():
         for p in range(3):
             own_weight(p).wait()
-        own_start(range(CHUNKS // 2))
-
-    tok_start(0, 1, 2)
-    tok_start(0, 0, 4)
-
-    @pl.when(owner)
-    def _():
-        own_start(range(CHUNKS // 2, CHUNKS))
-
-    tok_start(0, 0, 1)
-    tok_start(0, 1, 1)
+        own_start(range(CHUNKS))
+
+    for p, d in ((0, 2), (1, 4), (1, 2), (0, 4), (0, 1), (1, 1)):
+        tok_start(0, p, d)
 
     inner = jnp.logical_and(f > 0, f < n_fsdp - 1)
 
@@ -247,13 +237,38 @@
 
     t_pos = lax.broadcasted_iota(jnp.int32, (rows, rows), 0)
     u_pos = lax.broadcasted_iota(jnp.int32, (rows, rows), 1)
+    def add_up():
+        for r in range(1, CUBE):
+            pltpu.make_async_remote_copy(
+                src_ref=decay_in.at[0],
+                dst_ref=cums.at[flip(c, r)],
+                send_sem=cum_send.at[r],
+                recv_sem=cum_recv.at[r],
+                device_id={"ctx": flip(c, r)},
+                device_id_type=MESH,
+            ).wait_recv()
+
+        upto = jnp.where(t_pos <= u_pos, 1.0, 0.0).astype(F32)
+        for i in range(per_dev):
+            rates = jnp.concatenate(
+                [cums[b, pl.ds(head_of(c, i), 1), :] for b in range(CUBE)], axis=0
+            )
+            sums[i] = jnp.dot(
+                rates, upto, preferred_element_type=F32, precision=lax.Precision.HIGHEST
+            )
+
+    def decays_of(i, b):
+        row = sums[i, pl.ds(b, 1), :]
+        col = jnp.sum(jnp.where(t_pos == u_pos, row, 0.0), axis=1, keepdims=True)
+        inside = jnp.exp(jnp.where(t_pos >= u_pos, col - row, -jnp.inf))
+        return inside, jnp.exp(col), jnp.exp(row[:, rows - 1 :] - col)
+
     def decays(n, _):
         i, b = n // CUBE, n % CUBE
-        row = sums[i, pl.ds(b, 1), :]
-        col = jnp.sum(jnp.where(t_pos == u_pos, row, 0.0), axis=1, keepdims=True)
-        factors[i, b] = jnp.exp(jnp.where(t_pos >= u_pos, col - row, -jnp.inf))
-        opening[i, b] = jnp.broadcast_to(jnp.exp(col), (rows, hd))
-        closing[i, b] = jnp.broadcast_to(jnp.exp(row[:, rows - 1 :] - col), (rows, hd))
+        inside, opens, closes = decays_of(i, b)
+        factors[i, b] = inside
+        opening[i, b] = jnp.broadcast_to(opens, (rows, hd))
+        closing[i, b] = jnp.broadcast_to(closes, (rows, hd))
         return 0
 
     def activate(proj):
@@ -268,17 +283,17 @@
             bit *= 2
         return b
 
-    def block_alone(i, b, qkv):
+    def block_alone(qkv, factor, close):
         q, k, v = qkv[:, :hd], qkv[:, hd : 2 * hd], qkv[:, 2 * hd :]
         scores = lax.dot_general(q, k, (((1,), (1,)), ((), ())), preferred_element_type=F32)
-        weights = (scores * factors[i, b]).astype(BF16)
+        weights = (scores * factor).astype(BF16)
         inside = jnp.dot(weights, v, preferred_element_type=F32)
-        scaled = (k.astype(F32) * closing[i, b]).astype(BF16)
+        scaled = (k.astype(F32) * close).astype(BF16)
         local = lax.dot_general(scaled, v, (((0,), (0,)), ((), ())), preferred_element_type=F32)
         return inside, local
 
-    def chain(i, b, held, q, inside, local):
-        incoming = jnp.dot(q, held.astype(BF16), preferred_element_type=F32) * opening[i, b]
+    def chain(i, b, held, q, inside, local, opens):
+        incoming = jnp.dot(q, held.astype(BF16), preferred_element_type=F32) * opens
         total = jnp.exp(sums[i, pl.ds(b, 1), :][:, rows - 1 :])
         state[...] = total * held + local
         stage[i, b] = (inside + incoming).astype(BF16)
@@ -296,7 +311,7 @@
         b = flipped(r)
         qkv = activate(jnp.dot(tok[b], w[first], preferred_element_type=F32))
         near_q[b] = qkv[:, :hd]
-        near_inside[b], near_local[b] = block_alone(first, b, qkv)
+        near_inside[b], near_local[b] = block_alone(qkv, factors[first, b], closing[first, b])
         return 0
 
     def piece(b, lo, hi):
@@ -305,11 +320,6 @@
 
     half_way, most = CHUNKS // 2, CHUNKS - CHUNKS // 4
 
-    def grow(r, _):
-        b = flipped(r)
-        partial[b] = piece(b, 0, most)
-        return 0
-
     def grow_first(b, _):
         partial[b] = piece(b, 0, half_way)
         return 0
@@ -320,6 +330,75 @@
 
     def finish(b):
         far_qkv[b % 2] = activate(partial[b] + piece(b, most, CHUNKS))
+
+    def end_plane():
+        lax.fori_loop(6, CUBE, near_block, 0)
+
+        state[...] = jnp.zeros_like(state)
+
+        def near_one(b, _):
+            given = near_q[b], near_inside[b], near_local[b], opening[first, b]
+            chain(first, b, state[...], *given)
+            send(first, b)
+            return 0
+
+        lax.fori_loop(0, CUBE, near_one, 0)
+
+        end_wait(far, range(half_way))
+        lax.fori_loop(0, CUBE, grow_first, 0)
+        end_wait(far, range(half_way, most))
+        lax.fori_loop(0, CUBE, grow_next, 0)
+        end_wait(far, range(most, CHUNKS))
+
+        finish(0)
+        state[...] = jnp.zeros_like(state)
+
+        def far_block(b, ahead):
+            qkv, held = far_qkv[b % 2], state[...]
+            if ahead:
+                finish(b + 1)
+            inside, local = block_alone(qkv, factors[far, b], closing[far, b])
+            chain(far, b, held, qkv[:, :hd], inside, local, opening[far, b])
+            send(far, b)
+
+        def far_one(b, _):
+            far_block(b, True)
+            return 0
+
+        lax.fori_loop(0, CUBE - 1, far_one, 0)
+        far_block(CUBE - 1, False)
+
+    def place(t):
+        return first + (1 - 2 * first) * (t // CUBE), t % CUBE
+
+    def project(t):
+        i, b = place(t)
+        return jnp.dot(tok[b], w[i], preferred_element_type=F32)
+
+    def inner_block(t, ahead):
+        i, b = place(t)
+
+        @pl.when(b == 0)
+        def _():
+            state[...] = jnp.zeros_like(state)
+
+        qkv, held = far_qkv[t % 2], state[...]
+        proj = project(t + 1) if ahead else None
+        factor, opens, closes = decays_of(i, b)
+        inside, local = block_alone(qkv, factor, closes)
+        chain(i, b, held, qkv[:, :hd], inside, local, opens)
+        if ahead:
+            far_qkv[(t + 1) % 2] = activate(proj)
+        send(i, b)
+
+    def inner_one(t, _):
+        inner_block(t, True)
+        return 0
+
+    def inner_plane():
+        far_qkv[0] = activate(project(0))
+        lax.fori_loop(0, per_dev * CUBE - 1, inner_one, 0)
+        inner_block(per_dev * CUBE - 1, False)
 
     inner_pass(first, early)
     tok_wait(2, 0)
@@ -328,26 +407,11 @@
     tok_wait(4, 1)
     tok_start(4, 1, 2)
     tok_start(4, 1, 1)
-    for r in range(1, CUBE):
-        pltpu.make_async_remote_copy(
-            src_ref=decay_in.at[0],
-            dst_ref=cums.at[flip(c, r)],
-            send_sem=cum_send.at[r],
-            recv_sem=cum_recv.at[r],
-            device_id={"ctx": flip(c, r)},
-            device_id_type=MESH,
-        ).wait_recv()
-
-    upto = jnp.where(t_pos <= u_pos, 1.0, 0.0).astype(F32)
-    for i in range(per_dev):
-        rates = jnp.concatenate(
-            [cums[b, pl.ds(head_of(c, i), 1), :] for b in range(CUBE)], axis=0
-        )
-        sums[i] = jnp.dot(
-            rates, upto, preferred_element_type=F32, precision=lax.Precision.HIGHEST
-        )
-
-    lax.fori_loop(0, per_dev * CUBE, decays, 0)
+    @pl.when(jnp.logical_not(inner))
+    def _():
+        add_up()
+        lax.fori_loop(0, per_dev * CUBE, decays, 0)
+
     inner_pass(first, late)
     inner_pass(far, early)
     tok_wait(2, 1)
@@ -359,11 +423,13 @@
     for r in (1, 3, 5):
         for p in (0, 1):
             tok_wait(r, p)
-    lax.fori_loop(0, 6, near_block, 0)
-
     @pl.when(inner)
     def _():
-        lax.fori_loop(0, 6, grow, 0)
+        add_up()
+
+    @pl.when(jnp.logical_not(inner))
+    def _():
+        lax.fori_loop(0, 6, near_block, 0)
 
     tok_wait(6, 0)
     tok_start(6, 0, 1)
@@ -371,46 +437,13 @@
     tok_start(6, 1, 1)
     for p in (0, 1):
         tok_wait(7, p)
-    lax.fori_loop(6, CUBE, near_block, 0)
-
-    state[...] = jnp.zeros_like(state)
-
-    def near_one(b, _):
-        chain(first, b, state[...], near_q[b], near_inside[b], near_local[b])
-        send(first, b)
-        return 0
-
-    lax.fori_loop(0, CUBE, near_one, 0)
+    @pl.when(jnp.logical_not(inner))
+    def _():
+        end_plane()
 
     @pl.when(inner)
     def _():
-        lax.fori_loop(6, CUBE, grow, 0)
-
-    @pl.when(jnp.logical_not(inner))
-    def _():
-        end_wait(far, range(half_way))
-        lax.fori_loop(0, CUBE, grow_first, 0)
-        end_wait(far, range(half_way, most))
-        lax.fori_loop(0, CUBE, grow_next, 0)
-        end_wait(far, range(most, CHUNKS))
-
-    finish(0)
-    state[...] = jnp.zeros_like(state)
-
-    def far_block(b, ahead):
-        qkv, held = far_qkv[b % 2], state[...]
-        if ahead:
-            finish(b + 1)
-        inside, local = block_alone(far, b, qkv)
-        chain(far, b, held, qkv[:, :hd], inside, local)
-        send(far, b)
-
-    def far_one(b, _):
-        far_block(b, True)
-        return 0
-
-    lax.fori_loop(0, CUBE - 1, far_one, 0)
-    far_block(CUBE - 1, False)
+        inner_plane()
 
     for copy in sent:
         copy.wait_send()

time: 73.2 us -> 72.9 us (level)
  no operation moved by 1% of the time
where the time goes in v5:
time: 72.9 us; the launch traced here: 72.2 us
  Pallas kernels  69.9 us (96%)
  local copies, waits for them, and re-layouts  2.3 us (3%)
    pallas_call x1, Pallas kernels, head_body(): pl.pallas_call(functools.partial(head_kernel, dims), out_shape=jax.ShapeD...  69.9 us
    unnamed x1, local copies, waits for them, and re-layouts  2.3 us

profile of v5, /device:TPU:7, one launch (start us, length us, event | category | flops | bytes accessed | tf_op | source)
XLA Modules:
  0.0 72.2 jit_solution(3362322092718891106)
XLA Ops:
  0.0 69.9 %shard_map.46 = bf16[1,256,2048]{2,1,0:T(8,128)(2,1)} custom-call(bf16[1,256,2048]{2,1,0:T(8,128)(2,1)} %tok_in.1, bf16[3,2048,512]{2,1,0:T(8,128)(2,1)} %w_in.1, f32[1,16,256]{2,1,0:T(8,128)} %decay_in.1, f32[1,2048]{1,0:T(1,128)} %bitcast.1), custom_call_target="tpu_custom_call" | custom-call | flops 6442450944 | bytes 8388608 | tf_op jit(solution)/shard_map/pallas_call | solution.py:497
  69.9 2.3 %copy.6 = bf16[1,256,2048]{2,1,0:T(8,128)(2,1)} copy(bf16[1,256,2048]{2,1,0:T(8,128)(2,1)} %shard_map.46) | data formatting | bytes 2097152

commit v6 on v5

--- a/solution.py
+++ b/solution.py
@@ -414,11 +414,11 @@
 
     inner_pass(first, late)
     inner_pass(far, early)
+    inner_pass(far, late)
     tok_wait(2, 1)
     tok_start(2, 1, 1)
     tok_wait(4, 0)
     tok_start(4, 0, 1)
-    inner_pass(far, late)
     end_wait(first, range(CHUNKS))
     for r in (1, 3, 5):
         for p in (0, 1):

time: 72.9 us -> 72.9 us (level)
  no operation moved by 1% of the time
where the time goes in v6:
time: 72.9 us; the launch traced here: 72.2 us
  Pallas kernels  69.9 us (96%)
  local copies, waits for them, and re-layouts  2.3 us (3%)
    pallas_call x1, Pallas kernels, head_body(): pl.pallas_call(functools.partial(head_kernel, dims), out_shape=jax.ShapeD...  69.9 us
    unnamed x1, local copies, waits for them, and re-layouts  2.3 us

profile of v6, /device:TPU:7, one launch (start us, length us, event | category | flops | bytes accessed | tf_op | source)
XLA Modules:
  0.0 72.2 jit_solution(8678973169625441535)
XLA Ops:
  0.0 69.9 %shard_map.46 = bf16[1,256,2048]{2,1,0:T(8,128)(2,1)} custom-call(bf16[1,256,2048]{2,1,0:T(8,128)(2,1)} %tok_in.1, bf16[3,2048,512]{2,1,0:T(8,128)(2,1)} %w_in.1, f32[1,16,256]{2,1,0:T(8,128)} %decay_in.1, f32[1,2048]{1,0:T(1,128)} %bitcast.1), custom_call_target="tpu_custom_call" | custom-call | flops 6442450944 | bytes 8388608 | tf_op jit(solution)/shard_map/pallas_call | solution.py:497
  69.9 2.3 %copy.6 = bf16[1,256,2048]{2,1,0:T(8,128)(2,1)} copy(bf16[1,256,2048]{2,1,0:T(8,128)(2,1)} %shard_map.46) | data formatting | bytes 2097152
